TPU v7x, 256 devices: a whole 4x4x8 slice. The times are simulated.
256 devices in a mesh: outer: 4 (over y_hi, core), inner: 16 (over y_lo, z), head: 4 (over x).
Axes of the slice: x: 4, y: 4 (y_hi: 2, y_lo: 2; y = y_hi * 2 + y_lo), z: 8, core: 2. Of those that a mesh axis runs over, the one named last changes fastest.
Arguments:
- queries: bfloat16 [32768, 24, 128], P(('outer', 'inner', 'head')), may hold values from -6 to 6
- keys: bfloat16 [32768, 4, 128], P(('outer', 'inner', 'head')), may hold values from -6 to 6
- values: bfloat16 [32768, 4, 128], P(('outer', 'inner', 'head')), may hold values from -6 to 6
- block_order: int32 [128], replicated, may hold values from 0 to 127, each once
Outputs:
- attended: bfloat16 [32768, 24, 128], P(('outer', 'inner', 'head'))
- log_sum: float32 [24, 32768], P('head', ('outer', 'inner'))
Inputs may be any that keep to these rules, and one draw needn't show every extreme that they name: block_order names each half block once.
All inputs are finite; a program needn't handle non-finite values.
Results may differ from a plain program's by a relative error of at most 0.007.
Values may be sent and summed in bfloat16 or wider, within the bound.
A program may use at most 64 MiB of HBM per device.

v0:
```python
import math

import jax
import jax.numpy as jnp
from jax import lax
from jax.sharding import PartitionSpec as P


def shifted(x, axis, by):
    peers = lax.axis_size(axis)
    return lax.ppermute(x, axis, [(i, (i + by) % peers) for i in range(peers)])


def storage_positions(block_order, half_rows, first_row, row_total):
    row_ids = first_row + jnp.arange(row_total, dtype=jnp.int32)
    owners = row_ids // half_rows
    table = jnp.arange(block_order.shape[0], dtype=jnp.int32)
    picked = jnp.sum(jnp.where(owners[:, None] == table[None, :], block_order[None, :], 0), axis=1)
    return picked * half_rows + row_ids % half_rows


def attend_tile(carried, q_grouped, q_pos, k_tile, v_tile, k_pos, score_scale):
    running_max, totals, weighted = carried
    scores = (
        jnp.einsum("qhgd,khd->hgqk", q_grouped, k_tile, preferred_element_type=jnp.float32)
        * score_scale
    )
    visible = k_pos[None, :] <= q_pos[:, None]
    scores = jnp.where(visible, scores, -jnp.inf)
    new_max = jnp.maximum(running_max, jnp.max(scores, axis=-1))
    shrink = jnp.exp(running_max - new_max)
    powers = jnp.exp(scores - new_max[..., None])
    totals = totals * shrink + jnp.sum(powers, axis=-1)
    weighted = weighted * shrink[..., None] + jnp.einsum(
        "hgqk,khd->hgqd", powers.astype(jnp.bfloat16), v_tile, preferred_element_type=jnp.float32
    )
    return (new_max, totals, weighted)


def attend_span(
    carried,
    q_grouped,
    q_pos,
    k_span,
    v_span,
    first_row,
    block_order,
    half_rows,
    score_scale,
    tile_len,
):
    key_count = k_span.shape[0]
    piece_len = min(key_count, tile_len)
    tile_count = key_count // piece_len
    k_parts = k_span.reshape((tile_count, piece_len) + k_span.shape[1:])
    v_parts = v_span.reshape((tile_count, piece_len) + v_span.shape[1:])

    def advance(state, items):
        k_tile, v_tile, tile_id = items
        k_pos = storage_positions(
            block_order, half_rows, first_row + tile_id * piece_len, piece_len
        )
        state = attend_tile(state, q_grouped, q_pos, k_tile, v_tile, k_pos, score_scale)
        return (state, None)

    carried, _ = lax.scan(
        advance, carried, (k_parts, v_parts, jnp.arange(tile_count, dtype=jnp.int32))
    )
    return carried


def body(queries, keys, values, block_order):
    q_local, k_local, v_local = (
        lax.all_to_all(queries, "head", split_axis=1, concat_axis=0, tiled=True),
        lax.all_to_all(keys, "head", split_axis=1, concat_axis=0, tiled=True),
        lax.all_to_all(values, "head", split_axis=1, concat_axis=0, tiled=True),
    )
    row_count = q_local.shape[0]
    half_rows = row_count // 2
    kv_heads = k_local.shape[1]
    group = q_local.shape[1] // kv_heads
    head_dim = q_local.shape[2]
    score_scale = 1.0 / math.sqrt(head_dim)
    inner_count = lax.axis_size("inner")
    outer_count = lax.axis_size("outer")
    outer_here = lax.axis_index("outer")
    inner_here = lax.axis_index("inner")
    context = outer_here * inner_count + inner_here
    previous = (outer_here + outer_count - 1) % outer_count
    q_grouped = q_local.reshape(row_count, kv_heads, group, head_dim)
    q_pos = storage_positions(block_order, half_rows, context * row_count, row_count)
    running_max = jnp.full((kv_heads, group, row_count), -jnp.inf, jnp.float32)
    totals = jnp.zeros((kv_heads, group, row_count), jnp.float32)
    weighted = jnp.zeros((kv_heads, group, row_count, head_dim), jnp.float32)

    def absorb(state, k_span, v_span, first_row):
        return attend_span(
            state,
            q_grouped,
            q_pos,
            k_span,
            v_span,
            first_row,
            block_order,
            half_rows,
            score_scale,
            row_count,
        )

    def source_row(member):
        return (previous * inner_count + (member + 2 * inner_count) % inner_count) * row_count

    carried = absorb((running_max, totals, weighted), k_local, v_local, context * row_count)
    k_prev, v_prev = shifted((k_local, v_local), "outer", 1)
    carried = absorb(carried, k_prev, v_prev, source_row(inner_here))

    def turn(step_no, packed):
        state, k_now, v_now = packed
        k_now, v_now = shifted((k_now, v_now), "inner", 1)
        state = absorb(state, k_now, v_now, source_row(inner_here - step_no - 1))
        return (state, k_now, v_now)

    carried, k_last, v_last = lax.fori_loop(0, inner_count - 1, turn, (carried, k_prev, v_prev))
    running_max, totals, weighted = carried
    normalized = weighted / totals[..., None]
    out_rows = (
        jnp.transpose(normalized, (2, 0, 1, 3))
        .reshape(row_count, kv_heads * group, head_dim)
        .astype(jnp.bfloat16)
    )
    restored = lax.all_to_all(out_rows, "head", split_axis=0, concat_axis=1, tiled=True)
    log_rows = (running_max + jnp.log(totals)).reshape(kv_heads * group, row_count)
    return (restored, log_rows)


def solution(mesh):
    placed = (
        P(("outer", "inner", "head"), None, None),
        P(("outer", "inner", "head"), None, None),
        P(("outer", "inner", "head"), None, None),
        P(),
    )
    return jax.shard_map(
        body,
        mesh=mesh,
        in_specs=placed,
        out_specs=(P(("outer", "inner", "head"), None, None), P("head", ("outer", "inner"))),
        check_vma=False,
    )
```

profile of v0, /device:TPU:8, one launch (start us, length us, event | category | flops | bytes accessed | tf_op | source)
XLA Modules:
  0.0 275.4 jit_solution(3032697243405480675)
XLA Ops:
  2.2 4.3 %all-to-all-start = ((bf16[128,4,128]{2,0,1:T(8,128)(2,1)}), bf16[128,4,128]{2,0,1:T(8,128)(2,1)S(1)}, u32[]{:S(2)}, u32[]{:S(2)}) async-start(bf16[128,4,128]{2,0,1:T(8,128)(2,1)} %copy.51), calls=%async_computation | async-start | bytes 262144 | tf_op jit(solution)/shard_map/all_to_all | solution.py:75
  12.5 3.3 %all-to-all-start.2 = ((bf16[128,4,128]{2,0,1:T(8,128)(2,1)}), bf16[128,4,128]{2,0,1:T(8,128)(2,1)S(1)}, u32[]{:S(2)}, u32[]{:S(2)}) async-start(bf16[128,4,128]{2,0,1:T(8,128)(2,1)} %copy.54), calls=%async_computation.2 | async-start | bytes 262144 | tf_op jit(solution)/shard_map/all_to_all | solution.py:76
  16.8 4.9 %all-to-all-done.2 = bf16[128,4,128]{2,0,1:T(8,128)(2,1)S(1)} async-done(((bf16[128,4,128]{2,0,1:T(8,128)(2,1)}), bf16[128,4,128]{2,0,1:T(8,128)(2,1)S(1)}, u32[]{:S(2)}, u32[]{:S(2)}) %all-to-all-start.2) | async-done | bytes 131104 | tf_op jit(solution)/shard_map/all_to_all | solution.py:76
  21.7 3.5 %all-to-all-start.1 = ((bf16[128,24,128]{2,0,1:T(8,128)(2,1)}), bf16[128,24,128]{2,0,1:T(8,128)(2,1)S(1)}, u32[]{:S(2)}, u32[]{:S(2)}) async-start(bf16[128,24,128]{2,0,1:T(8,128)(2,1)} %copy.52), calls=%async_computation.1 | async-start | bytes 1572864 | tf_op jit(solution)/shard_map/all_to_all | solution.py:74
  28.1 7.1 %all-to-all-done.1 = bf16[128,24,128]{2,0,1:T(8,128)(2,1)S(1)} async-done(((bf16[128,24,128]{2,0,1:T(8,128)(2,1)}), bf16[128,24,128]{2,0,1:T(8,128)(2,1)S(1)}, u32[]{:S(2)}, u32[]{:S(2)}) %all-to-all-start.1) | async-done | bytes 786464 | tf_op jit(solution)/shard_map/all_to_all | solution.py:74
  44.8 210.9 %while.31 = (s32[]{:T(128)}, f32[1,6,512]{2,1,0:T(8,128)S(1)}, f32[1,6,512]{2,1,0:T(8,128)S(1)}, f32[1,6,512,128]{3,2,1,0:T(8,128)S(1)}, bf16[512,1,128]{2,0,1:T...) while((s32[]{:T(128)}, f32[1,6,512]{2,1,0:T(8,128)S(1)}, ...), condition=%wide.region_10.11_spmd, body=%wide.region_6.10_spmd.sunk | while | flops 823877120 | bytes 25901968 | solution.py:123
  49.2 5.8 %collective-permute-done = bf16[512,1,128]{2,0,1:T(8,128)(2,1)S(1)} collective-permute-done((bf16[512,1,128]{2,0,1:T(8,128)(2,1)S(1)}, bf16[512,1,128]{2,0,1:T(8,128)(2,1)S(1)}, u32[]{:S(2)}, u32[]{:S(2)}) %collective-permute-start) | collective-permute-done | bytes 131104 | tf_op jit(solution)/shard_map/while/body/eval_jaxpr/ppermute | solution.py:11
  61.7 6.7 %collective-permute-done = bf16[512,1,128]{2,0,1:T(8,128)(2,1)S(1)} collective-permute-done((bf16[512,1,128]{2,0,1:T(8,128)(2,1)S(1)}, bf16[512,1,128]{2,0,1:T(8,128)(2,1)S(1)}, u32[]{:S(2)}, u32[]{:S(2)}) %collective-permute-start) | collective-permute-done | bytes 131104 | tf_op jit(solution)/shard_map/while/body/eval_jaxpr/ppermute | solution.py:11
  74.2 7.6 %collective-permute-done = bf16[512,1,128]{2,0,1:T(8,128)(2,1)S(1)} collective-permute-done((bf16[512,1,128]{2,0,1:T(8,128)(2,1)S(1)}, bf16[512,1,128]{2,0,1:T(8,128)(2,1)S(1)}, u32[]{:S(2)}, u32[]{:S(2)}) %collective-permute-start) | collective-permute-done | bytes 131104 | tf_op jit(solution)/shard_map/while/body/eval_jaxpr/ppermute | solution.py:11
  87.3 7.9 %collective-permute-done = bf16[512,1,128]{2,0,1:T(8,128)(2,1)S(1)} collective-permute-done((bf16[512,1,128]{2,0,1:T(8,128)(2,1)S(1)}, bf16[512,1,128]{2,0,1:T(8,128)(2,1)S(1)}, u32[]{:S(2)}, u32[]{:S(2)}) %collective-permute-start) | collective-permute-done | bytes 131104 | tf_op jit(solution)/shard_map/while/body/eval_jaxpr/ppermute | solution.py:11
  100.7 7.9 %collective-permute-done = bf16[512,1,128]{2,0,1:T(8,128)(2,1)S(1)} collective-permute-done((bf16[512,1,128]{2,0,1:T(8,128)(2,1)S(1)}, bf16[512,1,128]{2,0,1:T(8,128)(2,1)S(1)}, u32[]{:S(2)}, u32[]{:S(2)}) %collective-permute-start) | collective-permute-done | bytes 131104 | tf_op jit(solution)/shard_map/while/body/eval_jaxpr/ppermute | solution.py:11
  114.3 8.3 %collective-permute-done = bf16[512,1,128]{2,0,1:T(8,128)(2,1)S(1)} collective-permute-done((bf16[512,1,128]{2,0,1:T(8,128)(2,1)S(1)}, bf16[512,1,128]{2,0,1:T(8,128)(2,1)S(1)}, u32[]{:S(2)}, u32[]{:S(2)}) %collective-permute-start) | collective-permute-done | bytes 131104 | tf_op jit(solution)/shard_map/while/body/eval_jaxpr/ppermute | solution.py:11
  128.2 9.6 %collective-permute-done = bf16[512,1,128]{2,0,1:T(8,128)(2,1)S(1)} collective-permute-done((bf16[512,1,128]{2,0,1:T(8,128)(2,1)S(1)}, bf16[512,1,128]{2,0,1:T(8,128)(2,1)S(1)}, u32[]{:S(2)}, u32[]{:S(2)}) %collective-permute-start) | collective-permute-done | bytes 131104 | tf_op jit(solution)/shard_map/while/body/eval_jaxpr/ppermute | solution.py:11
  143.3 10.6 %collective-permute-done = bf16[512,1,128]{2,0,1:T(8,128)(2,1)S(1)} collective-permute-done((bf16[512,1,128]{2,0,1:T(8,128)(2,1)S(1)}, bf16[512,1,128]{2,0,1:T(8,128)(2,1)S(1)}, u32[]{:S(2)}, u32[]{:S(2)}) %collective-permute-start) | collective-permute-done | bytes 131104 | tf_op jit(solution)/shard_map/while/body/eval_jaxpr/ppermute | solution.py:11
  159.5 9.7 %collective-permute-done = bf16[512,1,128]{2,0,1:T(8,128)(2,1)S(1)} collective-permute-done((bf16[512,1,128]{2,0,1:T(8,128)(2,1)S(1)}, bf16[512,1,128]{2,0,1:T(8,128)(2,1)S(1)}, u32[]{:S(2)}, u32[]{:S(2)}) %collective-permute-start) | collective-permute-done | bytes 131104 | tf_op jit(solution)/shard_map/while/body/eval_jaxpr/ppermute | solution.py:11
  174.7 8.9 %collective-permute-done = bf16[512,1,128]{2,0,1:T(8,128)(2,1)S(1)} collective-permute-done((bf16[512,1,128]{2,0,1:T(8,128)(2,1)S(1)}, bf16[512,1,128]{2,0,1:T(8,128)(2,1)S(1)}, u32[]{:S(2)}, u32[]{:S(2)}) %collective-permute-start) | collective-permute-done | bytes 131104 | tf_op jit(solution)/shard_map/while/body/eval_jaxpr/ppermute | solution.py:11
  189.2 8.0 %collective-permute-done = bf16[512,1,128]{2,0,1:T(8,128)(2,1)S(1)} collective-permute-done((bf16[512,1,128]{2,0,1:T(8,128)(2,1)S(1)}, bf16[512,1,128]{2,0,1:T(8,128)(2,1)S(1)}, u32[]{:S(2)}, u32[]{:S(2)}) %collective-permute-start) | collective-permute-done | bytes 131104 | tf_op jit(solution)/shard_map/while/body/eval_jaxpr/ppermute | solution.py:11
  202.7 7.9 %collective-permute-done = bf16[512,1,128]{2,0,1:T(8,128)(2,1)S(1)} collective-permute-done((bf16[512,1,128]{2,0,1:T(8,128)(2,1)S(1)}, bf16[512,1,128]{2,0,1:T(8,128)(2,1)S(1)}, u32[]{:S(2)}, u32[]{:S(2)}) %collective-permute-start) | collective-permute-done | bytes 131104 | tf_op jit(solution)/shard_map/while/body/eval_jaxpr/ppermute | solution.py:11
  216.1 7.9 %collective-permute-done = bf16[512,1,128]{2,0,1:T(8,128)(2,1)S(1)} collective-permute-done((bf16[512,1,128]{2,0,1:T(8,128)(2,1)S(1)}, bf16[512,1,128]{2,0,1:T(8,128)(2,1)S(1)}, u32[]{:S(2)}, u32[]{:S(2)}) %collective-permute-start) | collective-permute-done | bytes 131104 | tf_op jit(solution)/shard_map/while/body/eval_jaxpr/ppermute | solution.py:11
  229.5 7.9 %collective-permute-done = bf16[512,1,128]{2,0,1:T(8,128)(2,1)S(1)} collective-permute-done((bf16[512,1,128]{2,0,1:T(8,128)(2,1)S(1)}, bf16[512,1,128]{2,0,1:T(8,128)(2,1)S(1)}, u32[]{:S(2)}, u32[]{:S(2)}) %collective-permute-start) | collective-permute-done | bytes 131104 | tf_op jit(solution)/shard_map/while/body/eval_jaxpr/ppermute | solution.py:11
  242.9 7.9 %collective-permute-done = bf16[512,1,128]{2,0,1:T(8,128)(2,1)S(1)} collective-permute-done((bf16[512,1,128]{2,0,1:T(8,128)(2,1)S(1)}, bf16[512,1,128]{2,0,1:T(8,128)(2,1)S(1)}, u32[]{:S(2)}, u32[]{:S(2)}) %collective-permute-start) | collective-permute-done | bytes 131104 | tf_op jit(solution)/shard_map/while/body/eval_jaxpr/ppermute | solution.py:11
  255.8 3.6 %fusion.37 = bf16[512,6,128]{2,1,0:T(8,128)(2,1)} fusion(f32[6,512]{0,1:T(8,128)S(1)} %copy.58, f32[1,6,512,128]{3,2,1,0:T(8,128)S(1)} %get-tuple-element.505), kind=kLoop, calls=%fused_computation.52 | loop fusion | flops 786432 | bytes 2371584 | tf_op jit(solution)/shard_map/convert_element_type | solution.py:129
  259.4 3.5 %all-to-all-start.3 = ((bf16[512,6,128]{2,1,0:T(8,128)(2,1)}), bf16[512,6,128]{2,1,0:T(8,128)(2,1)S(1)}, u32[]{:S(2)}, u32[]{:S(2)}) async-start(bf16[512,6,128]{2,1,0:T(8,128)(2,1)} %fusion.37), calls=%async_computation.3 | async-start | bytes 2097152 | tf_op jit(solution)/shard_map/all_to_all | solution.py:131
  263.6 10.2 %all-to-all-done.3 = bf16[512,6,128]{2,1,0:T(8,128)(2,1)S(1)} async-done(((bf16[512,6,128]{2,1,0:T(8,128)(2,1)}), bf16[512,6,128]{2,1,0:T(8,128)(2,1)S(1)}, u32[]{:S(2)}, u32[]{:S(2)}) %all-to-all-start.3) | async-done | bytes 786464 | tf_op jit(solution)/shard_map/all_to_all | solution.py:131
  (253 shorter events, 109.9 us)
Async XLA Ops:
  2.2 10.3 %all-to-all-start = ((bf16[128,4,128]{2,0,1:T(8,128)(2,1)}), bf16[128,4,128]{2,0,1:T(8,128)(2,1)S(1)}, u32[]{:S(2)}, u32[]{:S(2)}) async-start(bf16[128,4,128]{2,0,1:T(8,128)(2,1)} %copy.51), calls=%async_computation | async-start | bytes 262144 | tf_op jit(solution)/shard_map/all_to_all | solution.py:75
  21.7 13.5 %all-to-all-start.1 = ((bf16[128,24,128]{2,0,1:T(8,128)(2,1)}), bf16[128,24,128]{2,0,1:T(8,128)(2,1)S(1)}, u32[]{:S(2)}, u32[]{:S(2)}) async-start(bf16[128,24,128]{2,0,1:T(8,128)(2,1)} %copy.52), calls=%async_computation.1 | async-start | bytes 1572864 | tf_op jit(solution)/shard_map/all_to_all | solution.py:74
  25.6 16.4 %collective-permute-start.3 = (bf16[512,1,128]{2,0,1:T(8,128)(2,1)S(1)}, bf16[512,1,128]{2,0,1:T(8,128)(2,1)S(1)}, u32[]{:S(2)}, u32[]{:S(2)}) collective-permute-start(bf16[512,1,128]{2,0,1:T(8,128)(2,1)S(1)} %bitcast.192), channel_id=1, source_target_pairs={{0,64},{64,128},{128,192},{192,0},{1,65},{65,129},{129,193},{193,1... | collective-permute-start | bytes 393224 | tf_op jit(solution)/shard_map/ppermute | solution.py:11
  25.7 13.7 %collective-permute-start.2 = (bf16[512,1,128]{2,0,1:T(8,128)(2,1)S(1)}, bf16[512,1,128]{2,0,1:T(8,128)(2,1)S(1)}, u32[]{:S(2)}, u32[]{:S(2)}) collective-permute-start(bf16[512,1,128]{2,0,1:T(8,128)(2,1)S(1)} %bitcast.190), channel_id=1, source_target_pairs={{0,64},{64,128},{128,192},{192,0},{1,65},{65,129},{129,193},{193,1... | collective-permute-start | bytes 393224 | tf_op jit(solution)/shard_map/ppermute | solution.py:11
  44.8 12.7 %collective-permute-start.1 = (bf16[512,1,128]{2,0,1:T(8,128)(2,1)S(1)}, bf16[512,1,128]{2,0,1:T(8,128)(2,1)S(1)}, u32[]{:S(2)}, u32[]{:S(2)}) collective-permute-start(bf16[512,1,128]{2,0,1:T(8,128)(2,1)S(1)} %get-tuple-element.654), channel_id=1, source_target_pairs={{0,4},{4,8},{8,12},{12,16},{16,20},{20,24},{24,28},{28,32},{32,36}... | collective-permute-start | bytes 393224 | tf_op jit(solution)/shard_map/while/body/eval_jaxpr/ppermute | solution.py:11
  59.8 11.1 %collective-permute-start.1 = (bf16[512,1,128]{2,0,1:T(8,128)(2,1)S(1)}, bf16[512,1,128]{2,0,1:T(8,128)(2,1)S(1)}, u32[]{:S(2)}, u32[]{:S(2)}) collective-permute-start(bf16[512,1,128]{2,0,1:T(8,128)(2,1)S(1)} %get-tuple-element.654), channel_id=1, source_target_pairs={{0,4},{4,8},{8,12},{12,16},{16,20},{20,24},{24,28},{28,32},{32,36}... | collective-permute-start | bytes 393224 | tf_op jit(solution)/shard_map/while/body/eval_jaxpr/ppermute | solution.py:11
  73.2 11.1 %collective-permute-start.1 = (bf16[512,1,128]{2,0,1:T(8,128)(2,1)S(1)}, bf16[512,1,128]{2,0,1:T(8,128)(2,1)S(1)}, u32[]{:S(2)}, u32[]{:S(2)}) collective-permute-start(bf16[512,1,128]{2,0,1:T(8,128)(2,1)S(1)} %get-tuple-element.654), channel_id=1, source_target_pairs={{0,4},{4,8},{8,12},{12,16},{16,20},{20,24},{24,28},{28,32},{32,36}... | collective-permute-start | bytes 393224 | tf_op jit(solution)/shard_map/while/body/eval_jaxpr/ppermute | solution.py:11
  86.6 11.1 %collective-permute-start.1 = (bf16[512,1,128]{2,0,1:T(8,128)(2,1)S(1)}, bf16[512,1,128]{2,0,1:T(8,128)(2,1)S(1)}, u32[]{:S(2)}, u32[]{:S(2)}) collective-permute-start(bf16[512,1,128]{2,0,1:T(8,128)(2,1)S(1)} %get-tuple-element.654), channel_id=1, source_target_pairs={{0,4},{4,8},{8,12},{12,16},{16,20},{20,24},{24,28},{28,32},{32,36}... | collective-permute-start | bytes 393224 | tf_op jit(solution)/shard_map/while/body/eval_jaxpr/ppermute | solution.py:11
  100.0 11.1 %collective-permute-start.1 = (bf16[512,1,128]{2,0,1:T(8,128)(2,1)S(1)}, bf16[512,1,128]{2,0,1:T(8,128)(2,1)S(1)}, u32[]{:S(2)}, u32[]{:S(2)}) collective-permute-start(bf16[512,1,128]{2,0,1:T(8,128)(2,1)S(1)} %get-tuple-element.654), channel_id=1, source_target_pairs={{0,4},{4,8},{8,12},{12,16},{16,20},{20,24},{24,28},{28,32},{32,36}... | collective-permute-start | bytes 393224 | tf_op jit(solution)/shard_map/while/body/eval_jaxpr/ppermute | solution.py:11
  113.5 11.7 %collective-permute-start.1 = (bf16[512,1,128]{2,0,1:T(8,128)(2,1)S(1)}, bf16[512,1,128]{2,0,1:T(8,128)(2,1)S(1)}, u32[]{:S(2)}, u32[]{:S(2)}) collective-permute-start(bf16[512,1,128]{2,0,1:T(8,128)(2,1)S(1)} %get-tuple-element.654), channel_id=1, source_target_pairs={{0,4},{4,8},{8,12},{12,16},{16,20},{20,24},{24,28},{28,32},{32,36}... | collective-permute-start | bytes 393224 | tf_op jit(solution)/shard_map/while/body/eval_jaxpr/ppermute | solution.py:11
  127.5 12.8 %collective-permute-start.1 = (bf16[512,1,128]{2,0,1:T(8,128)(2,1)S(1)}, bf16[512,1,128]{2,0,1:T(8,128)(2,1)S(1)}, u32[]{:S(2)}, u32[]{:S(2)}) collective-permute-start(bf16[512,1,128]{2,0,1:T(8,128)(2,1)S(1)} %get-tuple-element.654), channel_id=1, source_target_pairs={{0,4},{4,8},{8,12},{12,16},{16,20},{20,24},{24,28},{28,32},{32,36}... | collective-permute-start | bytes 393224 | tf_op jit(solution)/shard_map/while/body/eval_jaxpr/ppermute | solution.py:11
  127.6 10.2 %collective-permute-start = (bf16[512,1,128]{2,0,1:T(8,128)(2,1)S(1)}, bf16[512,1,128]{2,0,1:T(8,128)(2,1)S(1)}, u32[]{:S(2)}, u32[]{:S(2)}) collective-permute-start(bf16[512,1,128]{2,0,1:T(8,128)(2,1)S(1)} %get-tuple-element.653), channel_id=1, source_target_pairs={{0,4},{4,8},{8,12},{12,16},{16,20},{20,24},{24,28},{28,32},{32,36}... | collective-permute-start | bytes 393224 | tf_op jit(solution)/shard_map/while/body/eval_jaxpr/ppermute | solution.py:11
  142.6 13.8 %collective-permute-start.1 = (bf16[512,1,128]{2,0,1:T(8,128)(2,1)S(1)}, bf16[512,1,128]{2,0,1:T(8,128)(2,1)S(1)}, u32[]{:S(2)}, u32[]{:S(2)}) collective-permute-start(bf16[512,1,128]{2,0,1:T(8,128)(2,1)S(1)} %get-tuple-element.654), channel_id=1, source_target_pairs={{0,4},{4,8},{8,12},{12,16},{16,20},{20,24},{24,28},{28,32},{32,36}... | collective-permute-start | bytes 393224 | tf_op jit(solution)/shard_map/while/body/eval_jaxpr/ppermute | solution.py:11
  142.7 11.2 %collective-permute-start = (bf16[512,1,128]{2,0,1:T(8,128)(2,1)S(1)}, bf16[512,1,128]{2,0,1:T(8,128)(2,1)S(1)}, u32[]{:S(2)}, u32[]{:S(2)}) collective-permute-start(bf16[512,1,128]{2,0,1:T(8,128)(2,1)S(1)} %get-tuple-element.653), channel_id=1, source_target_pairs={{0,4},{4,8},{8,12},{12,16},{16,20},{20,24},{24,28},{28,32},{32,36}... | collective-permute-start | bytes 393224 | tf_op jit(solution)/shard_map/while/body/eval_jaxpr/ppermute | solution.py:11
  158.8 13.0 %collective-permute-start.1 = (bf16[512,1,128]{2,0,1:T(8,128)(2,1)S(1)}, bf16[512,1,128]{2,0,1:T(8,128)(2,1)S(1)}, u32[]{:S(2)}, u32[]{:S(2)}) collective-permute-start(bf16[512,1,128]{2,0,1:T(8,128)(2,1)S(1)} %get-tuple-element.654), channel_id=1, source_target_pairs={{0,4},{4,8},{8,12},{12,16},{16,20},{20,24},{24,28},{28,32},{32,36}... | collective-permute-start | bytes 393224 | tf_op jit(solution)/shard_map/while/body/eval_jaxpr/ppermute | solution.py:11
  158.8 10.3 %collective-permute-start = (bf16[512,1,128]{2,0,1:T(8,128)(2,1)S(1)}, bf16[512,1,128]{2,0,1:T(8,128)(2,1)S(1)}, u32[]{:S(2)}, u32[]{:S(2)}) collective-permute-start(bf16[512,1,128]{2,0,1:T(8,128)(2,1)S(1)} %get-tuple-element.653), channel_id=1, source_target_pairs={{0,4},{4,8},{8,12},{12,16},{16,20},{20,24},{24,28},{28,32},{32,36}... | collective-permute-start | bytes 393224 | tf_op jit(solution)/shard_map/while/body/eval_jaxpr/ppermute | solution.py:11
  174.0 12.1 %collective-permute-start.1 = (bf16[512,1,128]{2,0,1:T(8,128)(2,1)S(1)}, bf16[512,1,128]{2,0,1:T(8,128)(2,1)S(1)}, u32[]{:S(2)}, u32[]{:S(2)}) collective-permute-start(bf16[512,1,128]{2,0,1:T(8,128)(2,1)S(1)} %get-tuple-element.654), channel_id=1, source_target_pairs={{0,4},{4,8},{8,12},{12,16},{16,20},{20,24},{24,28},{28,32},{32,36}... | collective-permute-start | bytes 393224 | tf_op jit(solution)/shard_map/while/body/eval_jaxpr/ppermute | solution.py:11
  174.1 9.5 %collective-permute-start = (bf16[512,1,128]{2,0,1:T(8,128)(2,1)S(1)}, bf16[512,1,128]{2,0,1:T(8,128)(2,1)S(1)}, u32[]{:S(2)}, u32[]{:S(2)}) collective-permute-start(bf16[512,1,128]{2,0,1:T(8,128)(2,1)S(1)} %get-tuple-element.653), channel_id=1, source_target_pairs={{0,4},{4,8},{8,12},{12,16},{16,20},{20,24},{24,28},{28,32},{32,36}... | collective-permute-start | bytes 393224 | tf_op jit(solution)/shard_map/while/body/eval_jaxpr/ppermute | solution.py:11
  188.5 11.2 %collective-permute-start.1 = (bf16[512,1,128]{2,0,1:T(8,128)(2,1)S(1)}, bf16[512,1,128]{2,0,1:T(8,128)(2,1)S(1)}, u32[]{:S(2)}, u32[]{:S(2)}) collective-permute-start(bf16[512,1,128]{2,0,1:T(8,128)(2,1)S(1)} %get-tuple-element.654), channel_id=1, source_target_pairs={{0,4},{4,8},{8,12},{12,16},{16,20},{20,24},{24,28},{28,32},{32,36}... | collective-permute-start | bytes 393224 | tf_op jit(solution)/shard_map/while/body/eval_jaxpr/ppermute | solution.py:11
  202.0 11.1 %collective-permute-start.1 = (bf16[512,1,128]{2,0,1:T(8,128)(2,1)S(1)}, bf16[512,1,128]{2,0,1:T(8,128)(2,1)S(1)}, u32[]{:S(2)}, u32[]{:S(2)}) collective-permute-start(bf16[512,1,128]{2,0,1:T(8,128)(2,1)S(1)} %get-tuple-element.654), channel_id=1, source_target_pairs={{0,4},{4,8},{8,12},{12,16},{16,20},{20,24},{24,28},{28,32},{32,36}... | collective-permute-start | bytes 393224 | tf_op jit(solution)/shard_map/while/body/eval_jaxpr/ppermute | solution.py:11
  215.4 11.1 %collective-permute-start.1 = (bf16[512,1,128]{2,0,1:T(8,128)(2,1)S(1)}, bf16[512,1,128]{2,0,1:T(8,128)(2,1)S(1)}, u32[]{:S(2)}, u32[]{:S(2)}) collective-permute-start(bf16[512,1,128]{2,0,1:T(8,128)(2,1)S(1)} %get-tuple-element.654), channel_id=1, source_target_pairs={{0,4},{4,8},{8,12},{12,16},{16,20},{20,24},{24,28},{28,32},{32,36}... | collective-permute-start | bytes 393224 | tf_op jit(solution)/shard_map/while/body/eval_jaxpr/ppermute | solution.py:11
  228.8 11.1 %collective-permute-start.1 = (bf16[512,1,128]{2,0,1:T(8,128)(2,1)S(1)}, bf16[512,1,128]{2,0,1:T(8,128)(2,1)S(1)}, u32[]{:S(2)}, u32[]{:S(2)}) collective-permute-start(bf16[512,1,128]{2,0,1:T(8,128)(2,1)S(1)} %get-tuple-element.654), channel_id=1, source_target_pairs={{0,4},{4,8},{8,12},{12,16},{16,20},{20,24},{24,28},{28,32},{32,36}... | collective-permute-start | bytes 393224 | tf_op jit(solution)/shard_map/while/body/eval_jaxpr/ppermute | solution.py:11
  242.2 11.1 %collective-permute-start.1 = (bf16[512,1,128]{2,0,1:T(8,128)(2,1)S(1)}, bf16[512,1,128]{2,0,1:T(8,128)(2,1)S(1)}, u32[]{:S(2)}, u32[]{:S(2)}) collective-permute-start(bf16[512,1,128]{2,0,1:T(8,128)(2,1)S(1)} %get-tuple-element.654), channel_id=1, source_target_pairs={{0,4},{4,8},{8,12},{12,16},{16,20},{20,24},{24,28},{28,32},{32,36}... | collective-permute-start | bytes 393224 | tf_op jit(solution)/shard_map/while/body/eval_jaxpr/ppermute | solution.py:11
  259.4 14.4 %all-to-all-start.3 = ((bf16[512,6,128]{2,1,0:T(8,128)(2,1)}), bf16[512,6,128]{2,1,0:T(8,128)(2,1)S(1)}, u32[]{:S(2)}, u32[]{:S(2)}) async-start(bf16[512,6,128]{2,1,0:T(8,128)(2,1)} %fusion.37), calls=%async_computation.3 | async-start | bytes 2097152 | tf_op jit(solution)/shard_map/all_to_all | solution.py:131
  (13 other events, 105.6 us)
where the time goes:
time: 277 us; the launch traced here: 275 us
  waiting for transfers between devices  147 us (53%)
  matrix products  57.9 us (21%)
  other arithmetic  35.5 us (13%)
  starting transfers between devices  25.1 us (9%)
  local copies, waits for them, and re-layouts  7.46 us (3%)
    ppermute x32, waiting for transfers between devices, shifted(): return lax.ppermute(x, axis, [(i, (i + by) % peers) for i in range(peers)])  122 us
    dot_general x17, matrix products, attend_tile(): jnp.einsum('hgqk,khd->hgqd', powers.astype(jnp.bfloat16), v_tile, preferr...  38.2 us
    reduce_sum x17, other arithmetic, attend_tile(): totals = totals * shrink + jnp.sum(powers, axis=-1)  22.3 us
    dot_general x17, matrix products, attend_tile(): jnp.einsum('qhgd,khd->hgqk', q_grouped, k_tile, preferred_element_type=jn...  19.6 us
    ppermute x32, starting transfers between devices, shifted(): return lax.ppermute(x, axis, [(i, (i + by) % peers) for i in range(peers)])  10.5 us
    all_to_all x1, waiting for transfers between devices, body(): lax.all_to_all(out_rows, 'head', split_axis=0, concat_axis=1, tiled=True)  10.2 us
    all_to_all x1, waiting for transfers between devices, body(): lax.all_to_all(queries, 'head', split_axis=1, concat_axis=0, tiled=True)  7.06 us
    unnamed x6, local copies, waits for them, and re-layouts  6.72 us
  transfers between devices with their start and end apart: 36, of which 19 were waited for; matrix products, arithmetic and copies ran while one was open for 21% of the time, Pallas kernels for 0%

commit v1 on v0

v1 whole, which is shorter than its diff:
```python
import functools
import math

import jax
import jax.numpy as jnp
from jax import lax
from jax.experimental import pallas as pl
from jax.experimental.pallas import tpu as pltpu
from jax.sharding import PartitionSpec as P

MESH = pl.DeviceIdType.MESH
NEG = -1e30
LN2 = math.log(2.0)
NT = (((1,), (1,)), ((), ()))
NN = (((1,), (0,)), ((), ()))
ARRIVAL = (0, 1, 3, 2)
ORDER = (2, 1, 3, 0)


def kernel(
    group, ring, order_ref, q_in, kv_in, out_ref, log_ref,
    qbuf, own, kbuf, vbuf, outbuf, m_ref, acc_ref, s0, s1, tile_max,
    q_send, q_recv, x_send, x_recv, first_send, k_recv, v_recv, k_send, v_send, y_send,
    o_send, o_recv,
):
    outer, inner, head = (lax.axis_index(a) for a in ("outer", "inner", "head"))
    outers, heads = lax.axis_size("outer"), lax.axis_size("head")
    inners = lax.axis_size("inner")
    y, z = inner // ring, inner % ring
    part = q_in.shape[1] // group
    half = 2 * part
    keys = heads * part
    head_dim = q_in.shape[2]
    scale = math.log2(math.e) / math.sqrt(head_dim)
    core = outer % 2
    turn = 2 * core - 1
    after, before = (outer + 1) % outers, (outer + outers - 1) % outers
    near = jnp.where(core == 0, y, 1 - y)

    def at_head(by):
        return (outer, inner, (head + by) % heads)

    def at_next(y_there):
        return (after, y_there * ring + z, head)

    def at_z(by):
        return (outer, y * ring + (z + by + ring) % ring, head)

    y_peer = (outer, (1 - y) * ring + z, head)

    barrier = pltpu.get_barrier_semaphore()
    peers = [at_head(r) for r in (1, 2, 3)]
    peers += [at_next(0), at_next(1), (before, z, head), (before, ring + z, head)]
    peers += [at_z(1), at_z(-1), y_peer]
    for peer in peers:
        pl.semaphore_signal(barrier, inc=1, device_id=peer, device_id_type=MESH)
    pl.semaphore_wait(barrier, len(peers))

    def remote(src, dst, send, recv, peer):
        return pltpu.make_async_remote_copy(
            src_ref=src, dst_ref=dst, send_sem=send, recv_sem=recv,
            device_id=peer, device_id_type=MESH,
        )

    def kv_copy(r):
        there = (head + r) % heads
        return remote(kv_in.at[there], own.at[:, head], x_send.at[r], x_recv.at[r], at_head(r))

    def q_copy(r):
        there = (head + r) % heads
        return remote(q_in.at[there], qbuf.at[heads - r], q_send.at[r], q_recv.at[r], at_head(r))

    for r in (2, 1, 3):
        kv_copy(r).start()
    for r in (1, 3, 2):
        q_copy(r).start()
    own[0, head] = kv_in[head, 0]
    own[1, head] = kv_in[head, 1]
    qbuf[0] = q_in[head]
    m_ref[...] = jnp.full(m_ref.shape, NEG, jnp.float32)
    acc_ref[...] = jnp.zeros(acc_ref.shape, jnp.float32)
    for r in (1, 2, 3):
        kv_copy(r).wait_recv()

    def first_copies():
        return (
            remote(own.at[1], vbuf.at[0, z], first_send.at[0], v_recv.at[0, z], at_next(near)),
            remote(own.at[0], kbuf.at[0, z], first_send.at[1], k_recv.at[0, z], at_next(near)),
            remote(own.at[0], kbuf.at[1, z], first_send.at[2], k_recv.at[1, z], at_next(1 - near)),
        )

    for copy in first_copies():
        copy.start()

    def k_copy(way, kind, origin):
        peer = at_z(turn if way == 0 else -turn)
        return remote(
            kbuf.at[kind, origin], kbuf.at[kind, origin],
            k_send.at[way, kind, origin], k_recv.at[kind, origin], peer,
        )

    def v_copy(way, origin):
        peer = at_z(turn if way == 0 else -turn)
        return remote(
            vbuf.at[0, origin], vbuf.at[0, origin],
            v_send.at[way, origin], v_recv.at[0, origin], peer,
        )

    def y_copy(origin):
        return remote(
            vbuf.at[0, origin], vbuf.at[1, origin], y_send.at[origin], v_recv.at[1, origin], y_peer
        )

    def origin_of(way, step):
        by = turn * step
        return (z - by + ring) % ring if way == 0 else (z + by + ring) % ring

    def arrive_first():
        v_copy(0, z).wait_recv()
        v_copy(0, z).start()
        v_copy(1, z).start()
        y_copy(z).start()
        k_copy(0, 0, z).wait_recv()
        k_copy(0, 0, z).start()
        k_copy(1, 0, z).start()
        k_copy(0, 1, z).wait_recv()
        k_copy(0, 1, z).start()
        k_copy(1, 1, z).start()

    def last_step(way, kind):
        return ring // 2 if way == kind else ring // 2 - 1

    def arrive_from(way, kind, step, do):
        origin = origin_of(way, step)
        go = do == "go"
        onward = step < last_step(way, kind)
        if go:
            if kind == 0:
                v_copy(way, origin).wait_recv()
            k_copy(way, kind, origin).wait_recv()
        if kind == 0:
            if go:
                y_copy(origin).start()
            else:
                y_copy(origin).wait_send()

        def pass_on():
            if go:
                if kind == 0:
                    v_copy(way, origin).start()
                k_copy(way, kind, origin).start()
            else:
                if kind == 0:
                    v_copy(way, origin).wait_send()
                k_copy(way, kind, origin).wait_send()

        pl.when(onward)(pass_on)
        if go and kind == 1:
            remote(
                vbuf.at[1, origin], vbuf.at[1, origin], y_send.at[origin],
                v_recv.at[1, origin], y_peer,
            ).wait_recv()

    def arrive(c, do="go"):
        step, place = c // 4, c % 4
        for way in (0, 1):
            for kind in (0, 1):
                pl.when(place == 2 * kind + way)(
                    functools.partial(arrive_from, way, kind, step, do)
                )

    def slot_of(c):
        step, place = c // 4, c % 4
        kind = jnp.where(step == 0, place - 2, jnp.where(step == ring // 2, place, place // 2))
        sign = 1 - 2 * (place % 2)
        return kind, (z - turn * sign * step + ring) % ring

    def halves_of(c):
        kind, origin = slot_of(c)
        y_there = jnp.where((core + kind) % 2 == 1, y, 1 - y)
        block = before * inners + y_there * ring + origin
        return order_ref[2 * block], order_ref[2 * block + 1]

    here = 2 * (outer * inners + inner)
    here_order = (order_ref[here], order_ref[here + 1])

    def tile_order(r):
        return jnp.where((head + r) % heads < 2, here_order[0], here_order[1])

    scores = (s0, s1)
    columns = group * part

    def score(k_rows, r):
        q = qbuf[r]
        return lax.dot_general(k_rows, q, NT, preferred_element_type=jnp.float32) * scale

    def ahead(c, r, slot):
        kind, origin = slot_of(c)
        for h in range(2):
            k_rows = kbuf[kind, origin, 2 * h : 2 * h + 2].reshape(half, head_dim)
            s = score(k_rows, r)
            scores[slot][h * half : (h + 1) * half] = s
            tile_max[slot, h] = jnp.max(s, axis=0, keepdims=True)

    def ahead_own(r, slot):
        token = lax.broadcasted_iota(jnp.int32, (1, columns), 1) % part
        q_token = ((head + r) % 2) * part + token
        q_pos = tile_order(r) * half + q_token
        for h in range(2):
            k_rows = own[0, 2 * h : 2 * h + 2].reshape(half, head_dim)
            k_pos = here_order[h] * half + lax.broadcasted_iota(jnp.int32, (half, 1), 0)
            s = jnp.where(k_pos <= q_pos, score(k_rows, r), NEG)
            scores[slot][h * half : (h + 1) * half] = s
            tile_max[slot, h] = jnp.max(s, axis=0, keepdims=True)

    def absorb(v_parts, hidden, r, slot):
        old = m_ref[r]
        new = old
        for h in range(2):
            new = jnp.maximum(new, tile_max[slot, h] - hidden[h])
        shrink = jnp.exp2(old - new)
        m_ref[r] = new
        weights = jnp.concatenate(
            [
                jnp.exp2(scores[slot][h * half : (h + 1) * half] - (new + hidden[h]))
                for h in range(2)
            ],
            axis=0,
        ).astype(jnp.bfloat16)
        v = jnp.concatenate(v_parts, axis=1)
        v = jnp.concatenate([v, jnp.ones((16, keys), jnp.bfloat16)], axis=0)
        add = lax.dot_general(v, weights, NN, preferred_element_type=jnp.float32)
        acc_ref[r] = acc_ref[r] * shrink + add[: head_dim + 8]

    def now(c, r, slot):
        kind, origin = slot_of(c)
        mine = tile_order(r)
        hidden = [jnp.where(k < mine, 0.0, -NEG) for k in halves_of(c)]
        absorb([vbuf[kind, origin, x] for x in range(heads)], hidden, r, slot)

    def now_own(r, slot):
        absorb([own[1, x] for x in range(heads)], (0.0, 0.0), r, slot)

    def out_copy(r):
        return remote(
            outbuf.at[r], out_ref.at[head], o_send.at[r], o_recv.at[r], at_head(r)
        )

    def finish(r):
        total = acc_ref[r, head_dim : head_dim + 1]
        rows = (acc_ref[r, :head_dim] / total).T.astype(jnp.bfloat16)
        there = (head + r) % heads
        if r == 0:
            out_ref[head] = rows
        else:
            outbuf[r] = rows
            out_copy(r).start()
        logs = (m_ref[r] + jnp.log2(total)) * LN2
        for g in range(group):
            log_ref[g : g + 1, pl.ds(pl.multiple_of(there * part, part), part)] = logs[
                :, g * part : (g + 1) * part
            ]

    ahead_own(ARRIVAL[0], 0)
    for n, r in enumerate(ARRIVAL):
        if n == 1:
            arrive_first()
        if n < 3:
            q_copy(heads - ARRIVAL[n + 1]).wait_recv()
            ahead_own(ARRIVAL[n + 1], (n + 1) % 2)
        else:
            ahead(2, ORDER[0], 0)
        now_own(r, n % 2)

    remote(
        vbuf.at[1, z], vbuf.at[1, z], y_send.at[z], v_recv.at[1, z], y_peer
    ).wait_recv()

    def chunk(c, _):
        for n, r in enumerate(ORDER):
            if n == 2:
                pl.when(jnp.logical_and(c >= 3, c < 15))(lambda: arrive(c + 1))
                pl.when(c == 15)(lambda: arrive_from(0, 0, ring // 2, "go"))
            if n < 3:
                ahead(c, ORDER[n + 1], (n + 1) % 2)
            else:
                ahead(c + 1, ORDER[0], 0)
            now(c, r, n % 2)
        return 0

    lax.fori_loop(2, 16, chunk, 0)
    arrive_from(1, 1, ring // 2, "go")
    for n, r in enumerate(ORDER):
        ahead(17, r, 1)
        now(16, r, 0)
        if n < 3:
            ahead(16, ORDER[n + 1], 0)
        now(17, r, 1)
        finish(r)

    for r in (1, 2, 3):
        out_copy(r).wait_recv()
    for r in (1, 2, 3):
        out_copy(r).wait_send()
        kv_copy(r).wait_send()
        q_copy(r).wait_send()
    for copy in first_copies():
        copy.wait_send()
    y_copy(z).wait_send()
    for way in (0, 1):
        v_copy(way, z).wait_send()
        for kind in (0, 1):
            k_copy(way, kind, z).wait_send()

    def ended(c, _):
        arrive(c, "end")
        return 0

    lax.fori_loop(4, 16, ended, 0)
    y_copy(origin_of(0, ring // 2)).wait_send()


def body(queries, keys, values, block_order):
    heads = lax.axis_size("head")
    inners = lax.axis_size("inner")
    part, q_heads, head_dim = queries.shape
    group = q_heads // heads
    ring = inners // 2
    columns = group * part
    q_in = jnp.transpose(queries, (1, 0, 2)).reshape(heads, columns, head_dim)
    kv_in = jnp.stack([jnp.transpose(keys, (1, 0, 2)), jnp.transpose(values, (1, 2, 0))], axis=1)
    block = heads * part
    bf16, f32 = jnp.bfloat16, jnp.float32
    dma = pltpu.SemaphoreType.DMA
    vmem = pl.BlockSpec(memory_space=pltpu.VMEM)
    rows, logs = pl.pallas_call(
        functools.partial(kernel, group, ring),
        out_shape=(
            jax.ShapeDtypeStruct((heads, columns, head_dim), bf16),
            jax.ShapeDtypeStruct((group, block), f32),
        ),
        in_specs=[pl.BlockSpec(memory_space=pltpu.SMEM), vmem, vmem],
        out_specs=(vmem, vmem),
        scratch_shapes=[
            pltpu.VMEM((heads, columns, head_dim), bf16),
            pltpu.VMEM((2, heads, part, head_dim), bf16),
            pltpu.VMEM((2, ring, heads, part, head_dim), bf16),
            pltpu.VMEM((2, ring, heads, head_dim, part), bf16),
            pltpu.VMEM((heads, columns, head_dim), bf16),
            pltpu.VMEM((heads, 1, columns), f32),
            pltpu.VMEM((heads, head_dim + 8, columns), f32),
            pltpu.VMEM((block, columns), f32),
            pltpu.VMEM((block, columns), f32),
            pltpu.VMEM((2, 2, 1, columns), f32),
            dma((heads,)),
            dma((heads,)),
            dma((heads,)),
            dma((heads,)),
            dma((3,)),
            dma((2, ring)),
            dma((2, ring)),
            dma((2, 2, ring)),
            dma((2, ring)),
            dma((ring,)),
            dma((heads,)),
            dma((heads,)),
        ],
        compiler_params=pltpu.CompilerParams(
            collective_id=0, has_side_effects=True, vmem_limit_bytes=48 * 2**20
        ),
        cost_estimate=pl.CostEstimate(
            flops=4 * q_heads * block * (2 * ring + 1) * block * head_dim // heads,
            bytes_accessed=4 * 2**20,
            transcendentals=q_heads * block * (2 * ring + 1) * block // heads,
        ),
    )(block_order, q_in, kv_in)
    attended = jnp.transpose(rows.reshape(q_heads, part, head_dim), (1, 0, 2))
    return attended, logs


def solution(mesh):
    spread = P(("outer", "inner", "head"), None, None)
    return jax.shard_map(
        body,
        mesh=mesh,
        in_specs=(spread, spread, spread, P()),
        out_specs=(spread, P("head", ("outer", "inner"))),
        check_vma=False,
    )
```

time: 277 us -> 74.9 us (0.27)
  waiting for transfers between devices: 147 us -> 0 us
  Pallas kernels: 0 us -> 69.2 us
  matrix products: 57.9 us -> 0 us
  other arithmetic: 35.5 us -> 0.03 us
  starting transfers between devices: 25.1 us -> 0 us
    ppermute x32 -> x0, waiting for transfers between devices: 122 us -> none  [shifted(): return lax.ppermute(x, axis, [(i, (i + by) % peers) for i in range(peers)])]
    pallas_call x0 -> x1, Pallas kernels: none -> 69.2 us  [body(): pl.pallas_call(functools.partial(kernel, group, ring), out_shape=(jax.Sha...]
    dot_general x34 -> x0, matrix products: 57.9 us -> none  [the longest x17 38.2 us: attend_tile(): jnp.einsum('hgqk,khd->hgqd', powers.astype(jnp.bfloat16), v_tile, preferr...]
    reduce_sum x33 -> x0, other arithmetic: 26.8 us -> none  [the longest x17 22.3 us: attend_tile(): totals = totals * shrink + jnp.sum(powers, axis=-1)]
    all_to_all x4 -> x0, waiting for transfers between devices: 24.4 us -> none  [the longest x1 10.2 us: body(): lax.all_to_all(out_rows, 'head', split_axis=0, concat_axis=1, tiled=True)]
    all_to_all x4 -> x0, starting transfers between devices: 14.6 us -> none  [the longest x1 4.29 us: body(): lax.all_to_all(keys, 'head', split_axis=1, concat_axis=0, tiled=True)]
    ppermute x32 -> x0, starting transfers between devices: 10.5 us -> none  [shifted(): return lax.ppermute(x, axis, [(i, (i + by) % peers) for i in range(peers)])]
    convert_element_type x1 -> x0, other arithmetic: 3.61 us -> none  [body(): out_rows = jnp.transpose(normalized, (2, 0, 1, 3)).reshape(row_count, kv_...]
  transfers between devices with their start and end apart: 36 -> 0, of which waited for: 19 -> 0; matrix products, arithmetic and copies ran while one was open for 21% -> 0% of each run, Pallas kernels for 0% -> 0%
where the time goes in v1:
time: 74.9 us; the launch traced here: 74.8 us
  Pallas kernels  69.2 us (92%)
  local copies, waits for them, and re-layouts  4.84 us (6%)
    pallas_call x1, Pallas kernels, body(): pl.pallas_call(functools.partial(kernel, group, ring), out_shape=(jax.Sha...  69.2 us
    unnamed x7, local copies, waits for them, and re-layouts  3.29 us

profile of v1, /device:TPU:8, one launch (start us, length us, event | category | flops | bytes accessed | tf_op | source)
XLA Modules:
  0.0 74.8 jit_solution(15059454501274173470)
XLA Ops:
  0.6 0.0 copy-start.1
  0.6 1.0 %copy.13 = bf16[128,4,128]{2,0,1:T(8,128)(2,1)S(1)} copy(bf16[128,4,128]{2,1,0:T(4,128)(2,1)} %param.5) | data formatting | bytes 262144 | tf_op args[1]
  1.6 1.0 %copy.8 = bf16[128,4,128]{0,2,1:T(8,128)(2,1)S(1)} copy(bf16[128,4,128]{2,1,0:T(4,128)(2,1)} %param.6) | data formatting | bytes 262144 | tf_op args[2]
  2.7 0.0 copy-done.1
  2.7 0.2 copy.6
  2.9 0.0 copy-start
  2.9 0.6 copy-done
  3.6 69.2 %shard_map.59 = (bf16[4,768,128]{2,1,0:T(8,128)(2,1)S(1)}, f32[6,512]{1,0:T(8,128)S(1)}) custom-call(s32[128]{0:T(128)S(1)} %copy-done, bf16[4,768,128]{2,1,0:T(8,128)(2,1)S(1)} %bitcast.15, bf16[4,2,128,128]{3,2,1,0:T(8,128)(2,1)S(1)} %pad_maximum_fusion.kv_in), custom_call_target="tpu_custom_call" | custom-call | flops 13690208256 | bytes 4194304 | tf_op jit(solution)/shard_map/pallas_call | solution.py:336
  72.8 1.4 %copy.12 = bf16[24,128,128]{2,0,1:T(8,128)(2,1)} copy(bf16[24,128,128]{2,1,0:T(8,128)(2,1)S(1)} %bitcast.14) | data formatting | bytes 1572864 | tf_op jit(solution)/shard_map/reshape | solution.py:377
  74.2 0.6 copy.15
  (1 shorter events, 0.0 us)
Async XLA Ops:
  0.6 2.1 %copy-start.1 = (bf16[128,24,128]{2,1,0:T(8,128)(2,1)S(1)}, bf16[128,24,128]{2,1,0:T(8,128)(2,1)}, u32[]{:S(2)}) copy-start(bf16[128,24,128]{2,1,0:T(8,128)(2,1)} %param.4) | copy-start | bytes 2359300
  2.9 0.7 copy-start

commit v2 on v1

--- a/solution.py
+++ b/solution.py
@@ -14,13 +14,15 @@
 NT = (((1,), (1,)), ((), ()))
 NN = (((1,), (0,)), ((), ()))
 ARRIVAL = (0, 1, 3, 2)
+LOOP = (1, 3, 0, 2)
 ORDER = (2, 1, 3, 0)
+K1_PLACE = 1
 
 
 def kernel(
     group, ring, order_ref, q_in, kv_in, out_ref, log_ref,
     qbuf, own, kbuf, vbuf, outbuf, m_ref, acc_ref, s0, s1, tile_max,
-    q_send, q_recv, x_send, x_recv, first_send, k_recv, v_recv, k_send, v_send, y_send,
+    q_send, q_recv, x_send, x_recv, first_send, first_recv, k_recv, v_recv, k_send, v_send, y_send,
     o_send, o_recv,
 ):
     outer, inner, head = (lax.axis_index(a) for a in ("outer", "inner", "head"))
@@ -70,27 +72,25 @@
         there = (head + r) % heads
         return remote(q_in.at[there], qbuf.at[heads - r], q_send.at[r], q_recv.at[r], at_head(r))
 
-    for r in (2, 1, 3):
+    for r in (1, 3, 2):
         kv_copy(r).start()
     for r in (1, 3, 2):
         q_copy(r).start()
-    own[0, head] = kv_in[head, 0]
-    own[1, head] = kv_in[head, 1]
-    qbuf[0] = q_in[head]
-    m_ref[...] = jnp.full(m_ref.shape, NEG, jnp.float32)
-    acc_ref[...] = jnp.zeros(acc_ref.shape, jnp.float32)
-    for r in (1, 2, 3):
-        kv_copy(r).wait_recv()
-
-    def first_copies():
-        return (
-            remote(own.at[1], vbuf.at[0, z], first_send.at[0], v_recv.at[0, z], at_next(near)),
-            remote(own.at[0], kbuf.at[0, z], first_send.at[1], k_recv.at[0, z], at_next(near)),
-            remote(own.at[0], kbuf.at[1, z], first_send.at[2], k_recv.at[1, z], at_next(1 - near)),
-        )
-
-    for copy in first_copies():
-        copy.start()
+
+    def first_copy(r, n):
+        p = (head + r) % heads
+        src, dst, y_there = (
+            (own.at[1, p], vbuf.at[0, z, p], near),
+            (own.at[0, p], kbuf.at[0, z, p], near),
+            (own.at[0, p], kbuf.at[1, z, p], 1 - near),
+        )[n]
+        return remote(src, dst, first_send.at[n, r], first_recv.at[n, p], at_next(y_there))
+
+    def send_first(r):
+        if r:
+            kv_copy(heads - r).wait_recv()
+        for n in range(3):
+            first_copy(r, n).start()
 
     def k_copy(way, kind, origin):
         peer = at_z(turn if way == 0 else -turn)
@@ -115,59 +115,41 @@
         by = turn * step
         return (z - by + ring) % ring if way == 0 else (z + by + ring) % ring
 
-    def arrive_first():
-        v_copy(0, z).wait_recv()
-        v_copy(0, z).start()
-        v_copy(1, z).start()
-        y_copy(z).start()
-        k_copy(0, 0, z).wait_recv()
-        k_copy(0, 0, z).start()
-        k_copy(1, 0, z).start()
-        k_copy(0, 1, z).wait_recv()
-        k_copy(0, 1, z).start()
-        k_copy(1, 1, z).start()
+    def pass_first(r, ns):
+        p = (head + r) % heads
+        for n in ns:
+            first_copy(r, n).wait_recv()
+            for way in (0, 1):
+                peer = at_z(turn if way == 0 else -turn)
+                if n == 0:
+                    buf, send, recv = vbuf.at[0, z, p], v_send.at[way, z], v_recv.at[0, z]
+                else:
+                    buf = kbuf.at[n - 1, z, p]
+                    send, recv = k_send.at[way, n - 1, z], k_recv.at[n - 1, z]
+                remote(buf, buf, send, recv, peer).start()
 
     def last_step(way, kind):
         return ring // 2 if way == kind else ring // 2 - 1
 
-    def arrive_from(way, kind, step, do):
+    def v_event(way, step):
         origin = origin_of(way, step)
-        go = do == "go"
-        onward = step < last_step(way, kind)
-        if go:
-            if kind == 0:
-                v_copy(way, origin).wait_recv()
-            k_copy(way, kind, origin).wait_recv()
-        if kind == 0:
-            if go:
-                y_copy(origin).start()
-            else:
-                y_copy(origin).wait_send()
-
-        def pass_on():
-            if go:
-                if kind == 0:
-                    v_copy(way, origin).start()
-                k_copy(way, kind, origin).start()
-            else:
-                if kind == 0:
-                    v_copy(way, origin).wait_send()
-                k_copy(way, kind, origin).wait_send()
-
-        pl.when(onward)(pass_on)
-        if go and kind == 1:
-            remote(
-                vbuf.at[1, origin], vbuf.at[1, origin], y_send.at[origin],
-                v_recv.at[1, origin], y_peer,
-            ).wait_recv()
-
-    def arrive(c, do="go"):
-        step, place = c // 4, c % 4
-        for way in (0, 1):
-            for kind in (0, 1):
-                pl.when(place == 2 * kind + way)(
-                    functools.partial(arrive_from, way, kind, step, do)
-                )
+        v_copy(way, origin).wait_recv()
+        pl.when(step < last_step(way, 0))(lambda: v_copy(way, origin).start())
+        y_copy(origin).start()
+
+    def k_event(way, kind, step):
+        origin = origin_of(way, step)
+        k_copy(way, kind, origin).wait_recv()
+        pl.when(step < last_step(way, kind))(lambda: k_copy(way, kind, origin).start())
+
+    def k_events(kind, step):
+        k_event(0, kind, step)
+        k_event(1, kind, step)
+
+    def y_event(origin):
+        remote(
+            vbuf.at[1, origin], vbuf.at[1, origin], y_send.at[origin], v_recv.at[1, origin], y_peer
+        ).wait_recv()
 
     def slot_of(c):
         step, place = c // 4, c % 4
@@ -213,12 +195,12 @@
             scores[slot][h * half : (h + 1) * half] = s
             tile_max[slot, h] = jnp.max(s, axis=0, keepdims=True)
 
-    def absorb(v_parts, hidden, r, slot):
-        old = m_ref[r]
-        new = old
-        for h in range(2):
-            new = jnp.maximum(new, tile_max[slot, h] - hidden[h])
-        shrink = jnp.exp2(old - new)
+    def absorb(v_parts, hidden, r, slot, first=False):
+        new = jnp.maximum(tile_max[slot, 0] - hidden[0], tile_max[slot, 1] - hidden[1])
+        if not first:
+            old = m_ref[r]
+            new = jnp.maximum(old, new)
+            shrink = jnp.exp2(old - new)
         m_ref[r] = new
         weights = jnp.concatenate(
             [
@@ -230,7 +212,8 @@
         v = jnp.concatenate(v_parts, axis=1)
         v = jnp.concatenate([v, jnp.ones((16, keys), jnp.bfloat16)], axis=0)
         add = lax.dot_general(v, weights, NN, preferred_element_type=jnp.float32)
-        acc_ref[r] = acc_ref[r] * shrink + add[: head_dim + 8]
+        add = add[: head_dim + 8]
+        acc_ref[r] = add if first else acc_ref[r] * shrink + add
 
     def now(c, r, slot):
         kind, origin = slot_of(c)
@@ -239,7 +222,7 @@
         absorb([vbuf[kind, origin, x] for x in range(heads)], hidden, r, slot)
 
     def now_own(r, slot):
-        absorb([own[1, x] for x in range(heads)], (0.0, 0.0), r, slot)
+        absorb([own[1, x] for x in range(heads)], (0.0, 0.0), r, slot, first=True)
 
     def out_copy(r):
         return remote(
@@ -261,35 +244,85 @@
                 :, g * part : (g + 1) * part
             ]
 
-    ahead_own(ARRIVAL[0], 0)
-    for n, r in enumerate(ARRIVAL):
-        if n == 1:
-            arrive_first()
-        if n < 3:
-            q_copy(heads - ARRIVAL[n + 1]).wait_recv()
-            ahead_own(ARRIVAL[n + 1], (n + 1) % 2)
+    own[0, head] = kv_in[head, 0]
+    own[1, head] = kv_in[head, 1]
+    send_first(0)
+    qbuf[0] = q_in[head]
+    send_first(ARRIVAL[1])
+    pass_first(ARRIVAL[0], (0, 1))
+    send_first(ARRIVAL[2])
+    pass_first(ARRIVAL[1], (0, 1))
+    send_first(ARRIVAL[3])
+    pass_first(ARRIVAL[2], (0, 1))
+    pass_first(ARRIVAL[0], (2,))
+    pass_first(ARRIVAL[1], (2,))
+    pass_first(ARRIVAL[3], (0, 1))
+    y_copy(z).start()
+    pass_first(ARRIVAL[2], (2,))
+    pass_first(ARRIVAL[3], (2,))
+
+    def do_ahead(c, r, slot):
+        if c == 0:
+            if r:
+                q_copy(heads - r).wait_recv()
+            ahead_own(r, slot)
         else:
-            ahead(2, ORDER[0], 0)
-        now_own(r, n % 2)
-
-    remote(
-        vbuf.at[1, z], vbuf.at[1, z], y_send.at[z], v_recv.at[1, z], y_peer
-    ).wait_recv()
+            ahead(c, r, slot)
+
+    early = [(0, 0), (2, 0), (0, 1), (2, 1), (0, 3), (2, 3)]
+    early += [(3, 0), (3, 1), (3, 3), (0, 2), (2, 2), (3, 2)]
+    do_ahead(*early[0], 0)
+    for n in range(11):
+        if early[n + 1] == (0, 3):
+            v_event(0, 1)
+            v_event(1, 1)
+        if early[n + 1] == (0, 2):
+            k_events(0, 1)
+        do_ahead(*early[n + 1], (n + 1) % 2)
+        c, r = early[n]
+        if (c, r) == (3, 0):
+            y_event(z)
+        if c == 0:
+            now_own(r, n % 2)
+        else:
+            now(c, r, n % 2)
+
+    def events(c):
+        step, place = c // 4, c % 4
+
+        @pl.when(jnp.logical_and(place == 0, step > 1))
+        def _():
+            k_events(0, step)
+
+        @pl.when(place == K1_PLACE)
+        def _():
+            k_events(1, step)
+
+        @pl.when(place == 2)
+        def _():
+            y_event(origin_of(0, step))
+
+        @pl.when(place == 3)
+        def _():
+            y_event(origin_of(1, step))
+            v_event(0, step + 1)
+            pl.when(step < 3)(lambda: v_event(1, step + 1))
 
     def chunk(c, _):
-        for n, r in enumerate(ORDER):
-            if n == 2:
-                pl.when(jnp.logical_and(c >= 3, c < 15))(lambda: arrive(c + 1))
-                pl.when(c == 15)(lambda: arrive_from(0, 0, ring // 2, "go"))
-            if n < 3:
-                ahead(c, ORDER[n + 1], (n + 1) % 2)
-            else:
-                ahead(c + 1, ORDER[0], 0)
-            now(c, r, n % 2)
+        events(c)
+        ahead(c, LOOP[0], 0)
+        now(c - 1, LOOP[3], 1)
+        for n in range(3):
+            ahead(c, LOOP[n + 1], (n + 1) % 2)
+            now(c, LOOP[n], n % 2)
         return 0
 
-    lax.fori_loop(2, 16, chunk, 0)
-    arrive_from(1, 1, ring // 2, "go")
+    lax.fori_loop(4, 16, chunk, 0)
+    k_event(0, 0, ring // 2)
+    k_event(1, 1, ring // 2)
+    y_event(origin_of(0, ring // 2))
+    ahead(16, ORDER[0], 0)
+    now(15, LOOP[3], 1)
     for n, r in enumerate(ORDER):
         ahead(17, r, 1)
         now(16, r, 0)
@@ -304,19 +337,27 @@
         out_copy(r).wait_send()
         kv_copy(r).wait_send()
         q_copy(r).wait_send()
-    for copy in first_copies():
-        copy.wait_send()
+    for r in range(heads):
+        for n in range(3):
+            first_copy(r, n).wait_send()
     y_copy(z).wait_send()
     for way in (0, 1):
         v_copy(way, z).wait_send()
         for kind in (0, 1):
             k_copy(way, kind, z).wait_send()
 
-    def ended(c, _):
-        arrive(c, "end")
+    def ended(step, _):
+        for way in (0, 1):
+            origin = origin_of(way, step)
+            y_copy(origin).wait_send()
+            pl.when(step < last_step(way, 0))(lambda: v_copy(way, origin).wait_send())
+            for kind in (0, 1):
+                pl.when(step < last_step(way, kind))(
+                    lambda: k_copy(way, kind, origin).wait_send()
+                )
         return 0
 
-    lax.fori_loop(4, 16, ended, 0)
+    lax.fori_loop(1, 4, ended, 0)
     y_copy(origin_of(0, ring // 2)).wait_send()
 
 
@@ -356,7 +397,8 @@
             dma((heads,)),
             dma((heads,)),
             dma((heads,)),
-            dma((3,)),
+            dma((3, heads)),
+            dma((3, heads)),
             dma((2, ring)),
             dma((2, ring)),
             dma((2, 2, ring)),

time: 74.9 us -> 67.3 us (0.90); the launches traced: 74.8 us -> 66.3 us
  Pallas kernels: 69.2 us -> 60.8 us
    pallas_call x1, Pallas kernels: 69.2 us -> 60.8 us  [body(): pl.pallas_call(functools.partial(kernel, group, ring), out_shape=(jax.Sha...]
where the time goes in v2:
time: 67.3 us; the launch traced here: 66.3 us
  Pallas kernels  60.8 us (90%)
  local copies, waits for them, and re-layouts  4.84 us (7%)
  between operations  0.69 us (1%)
    pallas_call x1, Pallas kernels, body(): pl.pallas_call(functools.partial(kernel, group, ring), out_shape=(jax.Sha...  60.8 us
    unnamed x7, local copies, waits for them, and re-layouts  3.29 us
    reshape x1, local copies, waits for them, and re-layouts, body(): attended = jnp.transpose(rows.reshape(q_heads, part, head_dim), (1, 0, 2))  1.39 us

profile of v2, /device:TPU:8, one launch (start us, length us, event | category | flops | bytes accessed | tf_op | source)
XLA Modules:
  0.0 66.3 jit_solution(6694147549181910132)
XLA Ops:
  0.6 0.0 copy-start.1
  0.6 1.0 %copy.13 = bf16[128,4,128]{2,0,1:T(8,128)(2,1)S(1)} copy(bf16[128,4,128]{2,1,0:T(4,128)(2,1)} %param.5) | data formatting | bytes 262144 | tf_op args[1]
  1.6 1.0 %copy.8 = bf16[128,4,128]{0,2,1:T(8,128)(2,1)S(1)} copy(bf16[128,4,128]{2,1,0:T(4,128)(2,1)} %param.6) | data formatting | bytes 262144 | tf_op args[2]
  2.7 0.0 copy-done.1
  2.7 0.2 copy.6
  2.9 0.0 copy-start
  2.9 0.6 copy-done
  3.6 60.8 %shard_map.59 = (bf16[4,768,128]{2,1,0:T(8,128)(2,1)S(1)}, f32[6,512]{1,0:T(8,128)S(1)}) custom-call(s32[128]{0:T(128)S(1)} %copy-done, bf16[4,768,128]{2,1,0:T(8,128)(2,1)S(1)} %bitcast.15, bf16[4,2,128,128]{3,2,1,0:T(8,128)(2,1)S(1)} %pad_maximum_fusion.kv_in), custom_call_target="tpu_custom_call" | custom-call | flops 13690208256 | bytes 4194304 | tf_op jit(solution)/shard_map/pallas_call | solution.py:377
  64.3 1.4 %copy.12 = bf16[24,128,128]{2,0,1:T(8,128)(2,1)} copy(bf16[24,128,128]{2,1,0:T(8,128)(2,1)S(1)} %bitcast.14) | data formatting | bytes 1572864 | tf_op jit(solution)/shard_map/reshape | solution.py:419
  65.7 0.6 copy.15
  (1 shorter events, 0.0 us)
Async XLA Ops:
  0.6 2.1 %copy-start.1 = (bf16[128,24,128]{2,1,0:T(8,128)(2,1)S(1)}, bf16[128,24,128]{2,1,0:T(8,128)(2,1)}, u32[]{:S(2)}) copy-start(bf16[128,24,128]{2,1,0:T(8,128)(2,1)} %param.4) | copy-start | bytes 2359300
  2.9 0.7 copy-start

commit v3 on v2

--- a/solution.py
+++ b/solution.py
@@ -20,10 +20,10 @@
 
 
 def kernel(
-    group, ring, order_ref, q_in, kv_in, out_ref, log_ref,
-    qbuf, own, kbuf, vbuf, outbuf, m_ref, acc_ref, s0, s1, tile_max,
+    group, ring, order_in, q_hbm, k_hbm, v_hbm, out_ref, log_ref,
+    order_ref, q_ref, k_ref, v_ref, q_in, kv_in, got, qbuf, own, kbuf, vbuf, outbuf, m_ref, acc_ref, s0, s1, tile_max,
     q_send, q_recv, x_send, x_recv, first_send, first_recv, k_recv, v_recv, k_send, v_send, y_send,
-    o_send, o_recv,
+    o_send, o_recv, in_sem,
 ):
     outer, inner, head = (lax.axis_index(a) for a in ("outer", "inner", "head"))
     outers, heads = lax.axis_size("outer"), lax.axis_size("head")
@@ -49,6 +49,14 @@
         return (outer, y * ring + (z + by + ring) % ring, head)
 
     y_peer = (outer, (1 - y) * ring + z, head)
+    loads = [
+        pltpu.make_async_copy(src, dst, in_sem.at[n])
+        for n, (src, dst) in enumerate(
+            ((k_hbm, k_ref), (v_hbm, v_ref), (q_hbm, q_ref), (order_in, order_ref))
+        )
+    ]
+    for load in loads:
+        load.start()
 
     barrier = pltpu.get_barrier_semaphore()
     peers = [at_head(r) for r in (1, 2, 3)]
@@ -56,6 +64,12 @@
     peers += [at_z(1), at_z(-1), y_peer]
     for peer in peers:
         pl.semaphore_signal(barrier, inc=1, device_id=peer, device_id_type=MESH)
+    loads[0].wait()
+    loads[1].wait()
+    kv_in[:, 0] = jnp.swapaxes(k_ref[...], 0, 1)
+    v_rows = jnp.swapaxes(v_ref[...], 0, 1)
+    for x in range(heads):
+        kv_in[x, 1] = v_rows[x].T
     pl.semaphore_wait(barrier, len(peers))
 
     def remote(src, dst, send, recv, peer):
@@ -74,8 +88,11 @@
 
     for r in (1, 3, 2):
         kv_copy(r).start()
+    loads[2].wait()
+    q_in[...] = jnp.swapaxes(q_ref[...], 0, 1).reshape(q_in.shape)
     for r in (1, 3, 2):
         q_copy(r).start()
+    loads[3].wait()
 
     def first_copy(r, n):
         p = (head + r) % heads
@@ -226,7 +243,7 @@
 
     def out_copy(r):
         return remote(
-            outbuf.at[r], out_ref.at[head], o_send.at[r], o_recv.at[r], at_head(r)
+            outbuf.at[r], got.at[head], o_send.at[r], o_recv.at[r], at_head(r)
         )
 
     def finish(r):
@@ -234,7 +251,7 @@
         rows = (acc_ref[r, :head_dim] / total).T.astype(jnp.bfloat16)
         there = (head + r) % heads
         if r == 0:
-            out_ref[head] = rows
+            got[head] = rows
         else:
             outbuf[r] = rows
             out_copy(r).start()
@@ -333,6 +350,7 @@
 
     for r in (1, 2, 3):
         out_copy(r).wait_recv()
+    out_ref[...] = jnp.swapaxes(got[...].reshape(heads * group, part, head_dim), 0, 1)
     for r in (1, 2, 3):
         out_copy(r).wait_send()
         kv_copy(r).wait_send()
@@ -368,21 +386,26 @@
     group = q_heads // heads
     ring = inners // 2
     columns = group * part
-    q_in = jnp.transpose(queries, (1, 0, 2)).reshape(heads, columns, head_dim)
-    kv_in = jnp.stack([jnp.transpose(keys, (1, 0, 2)), jnp.transpose(values, (1, 2, 0))], axis=1)
     block = heads * part
     bf16, f32 = jnp.bfloat16, jnp.float32
     dma = pltpu.SemaphoreType.DMA
     vmem = pl.BlockSpec(memory_space=pltpu.VMEM)
-    rows, logs = pl.pallas_call(
+    return pl.pallas_call(
         functools.partial(kernel, group, ring),
         out_shape=(
-            jax.ShapeDtypeStruct((heads, columns, head_dim), bf16),
+            jax.ShapeDtypeStruct(queries.shape, bf16),
             jax.ShapeDtypeStruct((group, block), f32),
         ),
-        in_specs=[pl.BlockSpec(memory_space=pltpu.SMEM), vmem, vmem],
+        in_specs=[pl.BlockSpec(memory_space=pltpu.HBM)] * 4,
         out_specs=(vmem, vmem),
         scratch_shapes=[
+            pltpu.SMEM(block_order.shape, jnp.int32),
+            pltpu.VMEM(queries.shape, bf16),
+            pltpu.VMEM(keys.shape, bf16),
+            pltpu.VMEM(values.shape, bf16),
+            pltpu.VMEM((heads, columns, head_dim), bf16),
+            pltpu.VMEM((heads, 2, part, head_dim), bf16),
+            pltpu.VMEM((heads, columns, head_dim), bf16),
             pltpu.VMEM((heads, columns, head_dim), bf16),
             pltpu.VMEM((2, heads, part, head_dim), bf16),
             pltpu.VMEM((2, ring, heads, part, head_dim), bf16),
@@ -406,18 +429,17 @@
             dma((ring,)),
             dma((heads,)),
             dma((heads,)),
+            dma((4,)),
         ],
         compiler_params=pltpu.CompilerParams(
-            collective_id=0, has_side_effects=True, vmem_limit_bytes=48 * 2**20
+            collective_id=0, has_side_effects=True, vmem_limit_bytes=60 * 2**20
         ),
         cost_estimate=pl.CostEstimate(
             flops=4 * q_heads * block * (2 * ring + 1) * block * head_dim // heads,
             bytes_accessed=4 * 2**20,
             transcendentals=q_heads * block * (2 * ring + 1) * block // heads,
         ),
-    )(block_order, q_in, kv_in)
-    attended = jnp.transpose(rows.reshape(q_heads, part, head_dim), (1, 0, 2))
-    return attended, logs
+    )(block_order, queries, keys, values)
 
 
 def solution(mesh):

time: 67.3 us -> 65.8 us (0.978)
  local copies, waits for them, and re-layouts: 4.84 us -> 2.71 us
  Pallas kernels: 60.8 us -> 61.5 us
    reshape x1 -> x0, local copies, waits for them, and re-layouts: 1.39 us -> none  [body(): attended = jnp.transpose(rows.reshape(q_heads, part, head_dim), (1, 0, 2))]
    pallas_call x1, Pallas kernels: 60.8 us -> 61.5 us  [body(): pl.pallas_call(functools.partial(kernel, group, ring), out_shape=(jax.Sha...]
    unnamed x7 -> x4, local copies, waits for them, and re-layouts: 3.29 us -> 2.71 us
where the time goes in v3:
time: 65.8 us; the launch traced here: 64.8 us
  Pallas kernels  61.5 us (93%)
  local copies, waits for them, and re-layouts  2.71 us (4%)
    pallas_call x1, Pallas kernels, body(): pl.pallas_call(functools.partial(kernel, group, ring), out_shape=(jax.Sha...  61.5 us
    unnamed x4, local copies, waits for them, and re-layouts  2.71 us

profile of v3, /device:TPU:8, one launch (start us, length us, event | category | flops | bytes accessed | tf_op | source)
XLA Modules:
  0.0 64.8 jit_solution(11998567267230041550)
XLA Ops:
  0.6 61.5 %shard_map.59 = (bf16[128,24,128]{2,1,0:T(8,128)(2,1)}, f32[6,512]{1,0:T(8,128)}) custom-call(s32[128]{0:T(128)} %order_in.1, bf16[128,24,128]{2,1,0:T(8,128)(2,1)} %q_hbm.1, bf16[128,4,128]{2,1,0:T(4,128)(2,1)} %k_hbm.1, bf16[128,4,128]{2,1,0:T(4,128)(2,1)} %v_hbm.1), custom_call_target="tpu_custom_call" | custom-call | flops 13690208256 | bytes 4194304 | tf_op jit(solution)/shard_map/pallas_call | solution.py:393
  62.1 0.0 copy-start
  62.1 2.1 %copy.8 = bf16[128,24,128]{2,1,0:T(8,128)(2,1)} copy(bf16[128,24,128]{2,1,0:T(8,128)(2,1)} %get-tuple-element.4) | data formatting | bytes 1572864
  64.2 0.0 copy-done
  64.2 0.6 copy.9
Async XLA Ops:
  62.1 2.1 %copy-start = (f32[6,512]{1,0:T(8,128)S(1)}, f32[6,512]{1,0:T(8,128)}, u32[]{:S(2)}) copy-start(f32[6,512]{1,0:T(8,128)} %get-tuple-element.5) | copy-start | bytes 36868

commit v4 on v3

--- a/solution.py
+++ b/solution.py
@@ -16,6 +16,7 @@
 ARRIVAL = (0, 1, 3, 2)
 LOOP = (1, 3, 0, 2)
 ORDER = (2, 1, 3, 0)
+LAST = 16
 K1_PLACE = 1
 
 
@@ -248,7 +249,7 @@
 
     def finish(r):
         total = acc_ref[r, head_dim : head_dim + 1]
-        rows = (acc_ref[r, :head_dim] / total).T.astype(jnp.bfloat16)
+        rows = (acc_ref[r, :head_dim] / total).astype(jnp.bfloat16).T
         there = (head + r) % heads
         if r == 0:
             got[head] = rows
@@ -334,19 +335,31 @@
             now(c, LOOP[n], n % 2)
         return 0
 
-    lax.fori_loop(4, 16, chunk, 0)
-    k_event(0, 0, ring // 2)
-    k_event(1, 1, ring // 2)
-    y_event(origin_of(0, ring // 2))
-    ahead(16, ORDER[0], 0)
-    now(15, LOOP[3], 1)
-    for n, r in enumerate(ORDER):
-        ahead(17, r, 1)
-        now(16, r, 0)
-        if n < 3:
-            ahead(16, ORDER[n + 1], 0)
-        now(17, r, 1)
-        finish(r)
+    lax.fori_loop(4, LAST, chunk, 0)
+
+    if LAST < 15:
+        y_event(origin_of(0, 3))
+    if LAST < 16:
+        y_event(origin_of(1, 3))
+        v_event(0, 4)
+    steps = [(c, r) for r in ORDER for c in range(LAST, 18)]
+    last = len(steps) - 1
+    for n in range(-1, last + 1):
+        if n < last:
+            if steps[n + 1] == (16, ORDER[0]):
+                k_event(0, 0, ring // 2)
+            if steps[n + 1] == (17, ORDER[0]):
+                k_event(1, 1, ring // 2)
+            ahead(*steps[n + 1], (n + 1) % 2)
+        if n < 0:
+            now(LAST - 1, LOOP[3], 1)
+            continue
+        c, r = steps[n]
+        if (c, r) == (17, ORDER[0]):
+            y_event(origin_of(0, ring // 2))
+        now(c, r, n % 2)
+        if c == 17:
+            finish(r)
 
     for r in (1, 2, 3):
         out_copy(r).wait_recv()

time: 65.8 us -> 64.8 us (0.985)
  no operation moved by 1% of the time
where the time goes in v4:
time: 64.8 us; the launch traced here: 64.2 us
  Pallas kernels  60.9 us (94%)
  local copies, waits for them, and re-layouts  2.71 us (4%)
  between operations  0.65 us (1%)
    pallas_call x1, Pallas kernels, body(): pl.pallas_call(functools.partial(kernel, group, ring), out_shape=(jax.Sha...  60.9 us
    unnamed x4, local copies, waits for them, and re-layouts  2.71 us

profile of v4, /device:TPU:8, one launch (start us, length us, event | category | flops | bytes accessed | tf_op | source)
XLA Modules:
  0.0 64.2 jit_solution(12699774661604568960)
XLA Ops:
  0.6 60.9 %shard_map.59 = (bf16[128,24,128]{2,1,0:T(8,128)(2,1)}, f32[6,512]{1,0:T(8,128)}) custom-call(s32[128]{0:T(128)} %order_in.1, bf16[128,24,128]{2,1,0:T(8,128)(2,1)} %q_hbm.1, bf16[128,4,128]{2,1,0:T(4,128)(2,1)} %k_hbm.1, bf16[128,4,128]{2,1,0:T(4,128)(2,1)} %v_hbm.1), custom_call_target="tpu_custom_call" | custom-call | flops 13690208256 | bytes 4194304 | tf_op jit(solution)/shard_map/pallas_call | solution.py:406
  61.5 0.0 copy-start
  61.5 2.1 %copy.8 = bf16[128,24,128]{2,1,0:T(8,128)(2,1)} copy(bf16[128,24,128]{2,1,0:T(8,128)(2,1)} %get-tuple-element.4) | data formatting | bytes 1572864
  63.6 0.0 copy-done
  63.6 0.6 copy.9
Async XLA Ops:
  61.5 2.1 %copy-start = (f32[6,512]{1,0:T(8,128)S(1)}, f32[6,512]{1,0:T(8,128)}, u32[]{:S(2)}) copy-start(f32[6,512]{1,0:T(8,128)} %get-tuple-element.5) | copy-start | bytes 36868

commit v5 on v4

--- a/solution.py
+++ b/solution.py
@@ -242,20 +242,27 @@
     def now_own(r, slot):
         absorb([own[1, x] for x in range(heads)], (0.0, 0.0), r, slot, first=True)
 
-    def out_copy(r):
+    cut = columns // 2
+
+    def out_copy(r, n):
+        rows = pl.ds(n * cut, cut)
         return remote(
-            outbuf.at[r], got.at[head], o_send.at[r], o_recv.at[r], at_head(r)
+            outbuf.at[r, rows], got.at[head, rows], o_send.at[r, n], o_recv.at[r, n], at_head(r)
         )
 
     def finish(r):
         total = acc_ref[r, head_dim : head_dim + 1]
-        rows = (acc_ref[r, :head_dim] / total).astype(jnp.bfloat16).T
+        rows = [
+            (acc_ref[r, :head_dim, at : at + cut] / total[:, at : at + cut]).astype(jnp.bfloat16).T
+            for at in (0, cut)
+        ]
         there = (head + r) % heads
-        if r == 0:
-            got[head] = rows
-        else:
-            outbuf[r] = rows
-            out_copy(r).start()
+        for n in range(2):
+            if r == 0:
+                got[head, n * cut : (n + 1) * cut] = rows[n]
+            else:
+                outbuf[r, n * cut : (n + 1) * cut] = rows[n]
+                out_copy(r, n).start()
         logs = (m_ref[r] + jnp.log2(total)) * LN2
         for g in range(group):
             log_ref[g : g + 1, pl.ds(pl.multiple_of(there * part, part), part)] = logs[
@@ -362,10 +369,12 @@
             finish(r)
 
     for r in (1, 2, 3):
-        out_copy(r).wait_recv()
+        out_copy(r, 0).wait_recv()
+        out_copy(r, 1).wait_recv()
     out_ref[...] = jnp.swapaxes(got[...].reshape(heads * group, part, head_dim), 0, 1)
     for r in (1, 2, 3):
-        out_copy(r).wait_send()
+        out_copy(r, 0).wait_send()
+        out_copy(r, 1).wait_send()
         kv_copy(r).wait_send()
         q_copy(r).wait_send()
     for r in range(heads):
@@ -440,8 +449,8 @@
             dma((2, 2, ring)),
             dma((2, ring)),
             dma((ring,)),
-            dma((heads,)),
-            dma((heads,)),
+            dma((heads, 2)),
+            dma((heads, 2)),
             dma((4,)),
         ],
         compiler_params=pltpu.CompilerParams(

time: 64.8 us -> 64.8 us (level)
  no operation moved by 1% of the time
where the time goes in v5:
time: 64.8 us; the launch traced here: 64.3 us
  Pallas kernels  60.9 us (94%)
  local copies, waits for them, and re-layouts  2.71 us (4%)
  between operations  0.65 us (1%)
    pallas_call x1, Pallas kernels, body(): pl.pallas_call(functools.partial(kernel, group, ring), out_shape=(jax.Sha...  60.9 us
    unnamed x4, local copies, waits for them, and re-layouts  2.71 us

profile of v5, /device:TPU:8, one launch (start us, length us, event | category | flops | bytes accessed | tf_op | source)
XLA Modules:
  0.0 64.3 jit_solution(14810668872570548125)
XLA Ops:
  0.6 60.9 %shard_map.59 = (bf16[128,24,128]{2,1,0:T(8,128)(2,1)}, f32[6,512]{1,0:T(8,128)}) custom-call(s32[128]{0:T(128)} %order_in.1, bf16[128,24,128]{2,1,0:T(8,128)(2,1)} %q_hbm.1, bf16[128,4,128]{2,1,0:T(4,128)(2,1)} %k_hbm.1, bf16[128,4,128]{2,1,0:T(4,128)(2,1)} %v_hbm.1), custom_call_target="tpu_custom_call" | custom-call | flops 13690208256 | bytes 4194304 | tf_op jit(solution)/shard_map/pallas_call | solution.py:415
  61.6 0.0 copy-start
  61.6 2.1 %copy.8 = bf16[128,24,128]{2,1,0:T(8,128)(2,1)} copy(bf16[128,24,128]{2,1,0:T(8,128)(2,1)} %get-tuple-element.4) | data formatting | bytes 1572864
  63.7 0.0 copy-done
  63.7 0.6 copy.9
Async XLA Ops:
  61.6 2.1 %copy-start = (f32[6,512]{1,0:T(8,128)S(1)}, f32[6,512]{1,0:T(8,128)}, u32[]{:S(2)}) copy-start(f32[6,512]{1,0:T(8,128)} %get-tuple-element.5) | copy-start | bytes 36868
